TPU v7x, 128 devices: a whole 4x4x4 slice. The times are simulated.
128 devices in a mesh: sub: 16 (over x, y), ifc: 8 (over z, core).
Axes of the slice: x: 4, y: 4, z: 4, core: 2. Of those that a mesh axis runs over, the one named last changes fastest.
Arguments:
- schur: bfloat16 [512, 1536, 1536], P(('sub', 'ifc')), as said below
- lam_start: bfloat16 [6144, 64, 128], P(('sub', 'ifc')), may hold values from -6 to 6
- rhs: float32 [6144, 64, 128], P(('sub', 'ifc')), may hold values from -24 to 24
- stiff: float32 [6144, 64], P(('sub', 'ifc')), may hold values from 1 to 6
- owner: int32 [512, 24, 1], replicated, may hold values from 0 to 127; in each aligned block of 96 rows (0 to 95, 96 to 191, ..., all dimensions but the last counted through in order) at most 2 rows name the same one
- local: int32 [512, 24], replicated, may hold values from 0 to 47
Outputs:
- lam_final: float32 [6144, 64, 128], P(('sub', 'ifc'))
- sens: float32 [512, 128], P(('sub', 'ifc'))
Inputs may be any that keep to these rules, and one draw needn't show every extreme that they name: In the rows of one device (4 substructures of 24 slots) no owner is named more than 2 times, a bound that some block reaches. `schur`: each matrix is symmetric.
All inputs are finite; a program needn't handle non-finite values.
Results may differ from a plain program's by a relative error of at most 0.0008.
Values may be sent and summed in bfloat16 or wider, within the bound.
A program may use at most 128 MiB of HBM per device.

v0:
```python
import jax
import jax.numpy as jnp
from jax import lax
from jax.sharding import PartitionSpec as P

ITERS = 3


OMEGA = 0.7


def body(schur, lam_start, rhs, stiff, owner, local):
    ndev = lax.axis_size(("sub", "ifc"))
    me_index = lax.axis_index(("sub", "ifc"))
    sub_dev, order, _ = schur.shape
    if_dev, tile, width = lam_start.shape
    slots = owner.shape[1]
    per_dev = sub_dev * slots
    cap = max(2, 2 * per_dev // ndev)
    all_owner = owner[:, :, 0].reshape(ndev, per_dev)
    all_local = local.reshape(ndev, per_dev)
    mine = all_owner == me_index
    ranks = jnp.cumsum(mine.astype(jnp.int32), axis=1) - 1
    keyed = jnp.where(mine, ranks * if_dev + all_local, -1)
    target = jnp.arange(cap * if_dev, dtype=jnp.int32)
    select = jnp.any(keyed[:, :, None] == target[None, None, :], axis=1).reshape(ndev * cap, if_dev)
    own_owner = lax.dynamic_slice_in_dim(all_owner, me_index, 1, 0)[0]
    hits = own_owner[:, None] == jnp.arange(ndev, dtype=jnp.int32)[None, :]
    own_rank = jnp.sum(jnp.where(hits, jnp.cumsum(hits.astype(jnp.int32), axis=0) - 1, 0), axis=1)
    pick = (own_owner * cap + own_rank)[:, None] == jnp.arange(ndev * cap, dtype=jnp.int32)[None, :]
    pick_half = pick.astype(jnp.bfloat16)
    select_half = select.astype(jnp.bfloat16)
    diag_vals = jnp.diagonal(schur, axis1=1, axis2=2).astype(jnp.float32).reshape(per_dev, tile)
    diag_send = jnp.dot(pick.astype(jnp.float32).T, diag_vals, precision=lax.Precision.HIGHEST)
    diag_came = lax.all_to_all(
        diag_send.astype(jnp.bfloat16), ("sub", "ifc"), split_axis=0, concat_axis=0, tiled=True
    ).astype(diag_send.dtype)
    dsum = jnp.dot(select.astype(jnp.float32).T, diag_came, precision=lax.Precision.HIGHEST)
    dtotal = stiff + dsum
    lam = lam_start.astype(jnp.float32)
    gathered = None
    image = None
    for sweep in range(ITERS):
        lamb = lam.astype(jnp.bfloat16).reshape(if_dev, tile * width)
        send_tiles = jnp.dot(select_half, lamb, preferred_element_type=jnp.float32).astype(
            jnp.bfloat16
        )
        arrived = lax.all_to_all(
            send_tiles, ("sub", "ifc"), split_axis=0, concat_axis=0, tiled=True
        )
        gathered = jnp.dot(pick_half, arrived, preferred_element_type=jnp.float32).astype(
            jnp.bfloat16
        )
        gathered = gathered.reshape(sub_dev, order, width)
        image = jnp.einsum("sij,sjr->sir", schur, gathered, preferred_element_type=jnp.float32)
        rounded = image.astype(jnp.bfloat16).reshape(per_dev, tile * width)
        reply = jnp.dot(pick_half.T, rounded, preferred_element_type=jnp.float32).astype(
            jnp.bfloat16
        )
        returned = lax.all_to_all(reply, ("sub", "ifc"), split_axis=0, concat_axis=0, tiled=True)
        assembled = jnp.dot(select_half.T, returned, preferred_element_type=jnp.float32)
        assembled = assembled.reshape(if_dev, tile, width)
        resid = rhs - stiff[:, :, None] * lam - assembled
        lam = lam + OMEGA * resid / dtotal[:, :, None]
    sens = -jnp.sum(gathered.astype(jnp.float32) * image, axis=1) / order
    return (lam, sens)


def solution(mesh):
    return jax.shard_map(
        body,
        mesh=mesh,
        in_specs=(
            P(("sub", "ifc"), None, None),
            P(("sub", "ifc"), None, None),
            P(("sub", "ifc"), None, None),
            P(("sub", "ifc"), None),
            P(),
            P(),
        ),
        out_specs=(P(("sub", "ifc"), None, None), P(("sub", "ifc"), None)),
        check_vma=False,
    )
```

profile of v0, /device:TPU:1, one launch (start us, length us, event | category | flops | bytes accessed | tf_op | source)
XLA Modules:
  0.0 574.2 jit_solution(5706774296437403202)
XLA Ops:
  4.0 3.2 convolution_convert_fusion.2
  7.2 7.6 %all_to_all.56 = bf16[128,2,8192]{2,1,0:T(2,128)(2,1)} reshape(bf16[256,8192]{1,0:T(8,128)(2,1)} %convolution_convert_fusion.2) | data formatting | bytes 8388608 | tf_op jit(solution)/shard_map/all_to_all | solution.py:48
  14.8 12.0 %all-to-all-start = ((bf16[128,2,8192]{2,1,0:T(2,128)(2,1)}), bf16[128,2,8192]{2,1,0:T(2,128)(2,1)}, u32[]{:S(2)}, u32[]{:S(2)}) async-start(bf16[128,2,8192]{2,1,0:T(2,128)(2,1)} %all_to_all.56), calls=%async_computation | async-start | bytes 8388608 | tf_op jit(solution)/shard_map/all_to_all | solution.py:48
  27.0 24.8 %copy.65 = bf16[4,1536,1536]{2,0,1:T(4,128)(2,1)} copy(bf16[4,1536,1536]{2,1,0:T(8,128)(2,1)} %param.6) | data formatting | bytes 37748736 | tf_op args[0]
  51.9 18.2 %gather_fusion = bf16[1536,4]{0,1:T(4,128)(2,1)S(1)} fusion(bf16[4,1536,1536]{2,0,1:T(4,128)(2,1)} %copy.65, s32[1536]{0:T(1024)S(1)} %or_reduce_fusion), kind=kCustom, calls=%fused_computation | custom fusion | bytes 36864 | tf_op jit(solution)/shard_map/jit(diagonal)/gather | solution.py:33
  71.3 8.2 %all-to-all-done = bf16[128,2,8192]{2,1,0:T(2,128)(2,1)} async-done(((bf16[128,2,8192]{2,1,0:T(2,128)(2,1)}), bf16[128,2,8192]{2,1,0:T(2,128)(2,1)}, u32[]{:S(2)}, u32[]{:S(2)}) %all-to-all-start) | async-done | bytes 4194336 | tf_op jit(solution)/shard_map/all_to_all | solution.py:48
  79.6 5.4 all-to-all-start.2
  85.0 7.2 %all_to_all.58 = bf16[256,8192]{1,0:T(8,128)(2,1)} reshape(bf16[128,2,8192]{2,1,0:T(2,128)(2,1)} %all-to-all-done) | data formatting | bytes 8388608 | tf_op jit(solution)/shard_map/all_to_all | solution.py:48
  92.2 3.0 convolution_convert_fusion.8
  96.0 11.5 %fusion.1 = bf16[4,1536,128]{1,2,0:T(8,128)(2,1)} fusion(bf16[4,1536,128]{2,1,0:T(8,128)(2,1)S(1)} %reshape.98, bf16[4,1536,1536]{2,1,0:T(8,128)(2,1)} %param.6), kind=kOutput, calls=%fused_computation.16 | convolution fusion | flops 2416705536 | bytes 22020096 | tf_op jit(solution)/shard_map/sij,sjr->sir/dot_general | solution.py:55
  107.4 1.9 copy.62
  110.1 3.3 convolution_convert_fusion.5
  113.4 7.6 %all_to_all.59 = bf16[128,2,8192]{2,1,0:T(2,128)(2,1)} reshape(bf16[256,8192]{1,0:T(8,128)(2,1)} %convolution_convert_fusion.5) | data formatting | bytes 8388608 | tf_op jit(solution)/shard_map/all_to_all | solution.py:60
  121.0 10.2 %all-to-all-start.1 = ((bf16[128,2,8192]{2,1,0:T(2,128)(2,1)}), bf16[128,2,8192]{2,1,0:T(2,128)(2,1)}, u32[]{:S(2)}, u32[]{:S(2)}) async-start(bf16[128,2,8192]{2,1,0:T(2,128)(2,1)} %all_to_all.59), calls=%async_computation.1 | async-start | bytes 8388608 | tf_op jit(solution)/shard_map/all_to_all | solution.py:60
  131.6 52.4 %all-to-all-done.1 = bf16[128,2,8192]{2,1,0:T(2,128)(2,1)} async-done(((bf16[128,2,8192]{2,1,0:T(2,128)(2,1)}), bf16[128,2,8192]{2,1,0:T(2,128)(2,1)}, u32[]{:S(2)}, u32[]{:S(2)}) %all-to-all-start.1) | async-done | bytes 4194336 | tf_op jit(solution)/shard_map/all_to_all | solution.py:60
  184.1 7.2 %all_to_all.61 = bf16[256,8192]{1,0:T(8,128)(2,1)} reshape(bf16[128,2,8192]{2,1,0:T(2,128)(2,1)} %all-to-all-done.1) | data formatting | bytes 8388608 | tf_op jit(solution)/shard_map/all_to_all | solution.py:60
  191.2 6.6 %copy.63 = bf16[256,8192]{0,1:T(8,128)(2,1)} copy(bf16[256,8192]{1,0:T(8,128)(2,1)} %all_to_all.61) | data formatting | bytes 8388608 | tf_op jit(solution)/shard_map/all_to_all | solution.py:60
  197.8 6.1 %convert_add_fusion = f32[48,64,128]{2,0,1:T(8,128)S(1)} fusion(bf16[64,128,256]{2,1,0:T(8,128)(2,1)} %bitcast.81, f32[48,64,128]{2,1,0:T(8,128)S(1)} %copy-done.7, bf16[48,64,128]{2,1,0:T(8,128)(2,1)S(1)} %copy-done.5, f32[48,64]{0,1:T(8,128)S(1)} %copy.67, f32[48,64]{0,1:T(8,128)S(1)} %copy.54, pred[256,48]{1,0:T(32,128)(4,1)S(1)} %reshape.96), kind=kOutput, calls=%fused_computation.18 | convolution fusion | flops 204079104 | bytes 8163328 | tf_op jit(solution)/shard_map/dot_general | solution.py:61
  203.9 1.1 copy-done.2
  205.1 3.2 convolution_convert_fusion.1
  208.3 7.6 %all_to_all.65 = bf16[128,2,8192]{2,1,0:T(2,128)(2,1)} reshape(bf16[256,8192]{1,0:T(8,128)(2,1)} %convolution_convert_fusion.1) | data formatting | bytes 8388608 | tf_op jit(solution)/shard_map/all_to_all | solution.py:48
  215.9 59.0 %all_to_all.84 = bf16[128,2,8192]{2,1,0:T(2,128)(2,1)} all-to-all(bf16[128,2,8192]{2,1,0:T(2,128)(2,1)} %all_to_all.65), channel_id=1, replica_groups=mesh['sub'=16,'ifc'=8] {'sub','ifc'}, dimensions={0} | all-to-all | bytes 8388608 | tf_op jit(solution)/shard_map/all_to_all | solution.py:48
  274.9 7.2 %all_to_all.67 = bf16[256,8192]{1,0:T(8,128)(2,1)} reshape(bf16[128,2,8192]{2,1,0:T(2,128)(2,1)} %all_to_all.84) | data formatting | bytes 8388608 | tf_op jit(solution)/shard_map/all_to_all | solution.py:48
  282.0 3.0 convolution_convert_fusion.7
  285.9 11.5 %fusion.2 = bf16[4,1536,128]{1,2,0:T(8,128)(2,1)} fusion(bf16[4,1536,128]{2,1,0:T(8,128)(2,1)S(1)} %reshape.102, bf16[4,1536,1536]{2,1,0:T(8,128)(2,1)} %param.6), kind=kOutput, calls=%fused_computation.17 | convolution fusion | flops 2416705536 | bytes 22020096 | tf_op jit(solution)/shard_map/sij,sjr->sir/dot_general | solution.py:55
  297.4 1.9 copy.71
  300.0 3.3 convolution_convert_fusion.4
  303.3 7.6 %all_to_all.68 = bf16[128,2,8192]{2,1,0:T(2,128)(2,1)} reshape(bf16[256,8192]{1,0:T(8,128)(2,1)} %convolution_convert_fusion.4) | data formatting | bytes 8388608 | tf_op jit(solution)/shard_map/all_to_all | solution.py:60
  311.0 58.8 %all_to_all.85 = bf16[128,2,8192]{2,1,0:T(2,128)(2,1)} all-to-all(bf16[128,2,8192]{2,1,0:T(2,128)(2,1)} %all_to_all.68), channel_id=1, replica_groups=mesh['sub'=16,'ifc'=8] {'sub','ifc'}, dimensions={0} | all-to-all | bytes 8388608 | tf_op jit(solution)/shard_map/all_to_all | solution.py:60
  369.8 7.2 %all_to_all.70 = bf16[256,8192]{1,0:T(8,128)(2,1)} reshape(bf16[128,2,8192]{2,1,0:T(2,128)(2,1)} %all_to_all.85) | data formatting | bytes 8388608 | tf_op jit(solution)/shard_map/all_to_all | solution.py:60
  377.0 6.6 %copy.72 = bf16[256,8192]{0,1:T(8,128)(2,1)} copy(bf16[256,8192]{1,0:T(8,128)(2,1)} %all_to_all.70) | data formatting | bytes 8388608 | tf_op jit(solution)/shard_map/all_to_all | solution.py:60
  383.5 4.6 divide_add_fusion.1
  388.2 1.1 copy-done
  389.3 3.2 convolution_convert_fusion
  392.5 7.6 %all_to_all.71 = bf16[128,2,8192]{2,1,0:T(2,128)(2,1)} reshape(bf16[256,8192]{1,0:T(8,128)(2,1)} %convolution_convert_fusion) | data formatting | bytes 8388608 | tf_op jit(solution)/shard_map/all_to_all | solution.py:48
  400.1 59.0 %all_to_all.86 = bf16[128,2,8192]{2,1,0:T(2,128)(2,1)} all-to-all(bf16[128,2,8192]{2,1,0:T(2,128)(2,1)} %all_to_all.71), channel_id=1, replica_groups=mesh['sub'=16,'ifc'=8] {'sub','ifc'}, dimensions={0} | all-to-all | bytes 8388608 | tf_op jit(solution)/shard_map/all_to_all | solution.py:48
  459.1 7.2 %all_to_all.73 = bf16[256,8192]{1,0:T(8,128)(2,1)} reshape(bf16[128,2,8192]{2,1,0:T(2,128)(2,1)} %all_to_all.86) | data formatting | bytes 8388608 | tf_op jit(solution)/shard_map/all_to_all | solution.py:48
  466.3 3.0 convolution_convert_fusion.6
  470.1 1.6 copy.80
  471.7 11.0 %multiply_reduce_fusion = (f32[4,128]{1,0:T(4,128)S(1)}, bf16[4,1536,128]{1,2,0:T(8,128)(2,1)S(1)}) fusion(bf16[4,1536,128]{1,2,0:T(8,128)(2,1)} %copy.80, bf16[4,1536,128]{2,1,0:T(8,128)(2,1)S(1)} %reshape.105, bf16[4,1536,1536]{2,1,0:T(8,128)(2,1)} %param.6), kind=kOutput, calls=%fused_computation.13 | convolution fusion | flops 2419064320 | bytes 23595008 | tf_op jit(solution)/shard_map/sij,sjr->sir/dot_general | solution.py:55
  484.4 3.3 convolution_convert_fusion.3
  487.7 7.6 %all_to_all.74 = bf16[128,2,8192]{2,1,0:T(2,128)(2,1)} reshape(bf16[256,8192]{1,0:T(8,128)(2,1)} %convolution_convert_fusion.3) | data formatting | bytes 8388608 | tf_op jit(solution)/shard_map/all_to_all | solution.py:60
  495.3 5.7 %all-to-all-start.6 = ((bf16[128,2,8192]{2,1,0:T(2,128)(2,1)}), bf16[128,2,8192]{2,1,0:T(2,128)(2,1)}, u32[]{:S(2)}, u32[]{:S(2)}) async-start(bf16[128,2,8192]{2,1,0:T(2,128)(2,1)} %all_to_all.74), calls=%async_computation.6 | async-start | bytes 8388608 | tf_op jit(solution)/shard_map/all_to_all | solution.py:60
  501.7 52.3 %all-to-all-done.6 = bf16[128,2,8192]{2,1,0:T(2,128)(2,1)} async-done(((bf16[128,2,8192]{2,1,0:T(2,128)(2,1)}), bf16[128,2,8192]{2,1,0:T(2,128)(2,1)}, u32[]{:S(2)}, u32[]{:S(2)}) %all-to-all-start.6) | async-done | bytes 4194336 | tf_op jit(solution)/shard_map/all_to_all | solution.py:60
  553.9 7.2 %all_to_all.76 = bf16[256,8192]{1,0:T(8,128)(2,1)} reshape(bf16[128,2,8192]{2,1,0:T(2,128)(2,1)} %all-to-all-done.6) | data formatting | bytes 8388608 | tf_op jit(solution)/shard_map/all_to_all | solution.py:60
  561.2 6.5 %copy.78 = bf16[256,8192]{0,1:T(8,128)(2,1)} copy(bf16[256,8192]{1,0:T(8,128)(2,1)} %all_to_all.76) | data formatting | bytes 8388608 | tf_op jit(solution)/shard_map/all_to_all | solution.py:60
  567.7 4.6 divide_add_fusion
  572.4 1.6 copy.81
  (51 shorter events, 11.2 us)
Async XLA Ops:
  0.6 3.4 copy-start.4
  14.8 64.7 %all-to-all-start = ((bf16[128,2,8192]{2,1,0:T(2,128)(2,1)}), bf16[128,2,8192]{2,1,0:T(2,128)(2,1)}, u32[]{:S(2)}, u32[]{:S(2)}) async-start(bf16[128,2,8192]{2,1,0:T(2,128)(2,1)} %all_to_all.56), calls=%async_computation | async-start | bytes 8388608 | tf_op jit(solution)/shard_map/all_to_all | solution.py:48
  79.6 41.5 %all-to-all-start.2 = ((bf16[128,2,64]{2,1,0:T(2,128)(2,1)}), bf16[128,2,64]{2,1,0:T(2,128)(2,1)S(1)}, u32[]{:S(2)}, u32[]{:S(2)}) async-start(bf16[128,2,64]{2,1,0:T(2,128)(2,1)} %bitcast.6), calls=%async_computation.2 | async-start | bytes 131072 | tf_op jit(solution)/shard_map/all_to_all | solution.py:35
  121.0 10.2 %copy-start.6 = (f32[48,64]{1,0:T(8,128)S(1)}, f32[48,64]{1,0:T(8,128)}, u32[]{:S(2)}) copy-start(f32[48,64]{1,0:T(8,128)} %param.9) | copy-start | bytes 36868
  121.0 63.0 %all-to-all-start.1 = ((bf16[128,2,8192]{2,1,0:T(2,128)(2,1)}), bf16[128,2,8192]{2,1,0:T(2,128)(2,1)}, u32[]{:S(2)}, u32[]{:S(2)}) async-start(bf16[128,2,8192]{2,1,0:T(2,128)(2,1)} %all_to_all.59), calls=%async_computation.1 | async-start | bytes 8388608 | tf_op jit(solution)/shard_map/all_to_all | solution.py:60
  191.2 6.6 %copy-start.5 = (bf16[48,64,128]{2,1,0:T(8,128)(2,1)S(1)}, bf16[48,64,128]{2,1,0:T(8,128)(2,1)}, u32[]{:S(2)}) copy-start(bf16[48,64,128]{2,1,0:T(8,128)(2,1)} %param.7) | copy-start | bytes 2359300
  191.2 6.6 %copy-start.7 = (f32[48,64,128]{2,1,0:T(8,128)S(1)}, f32[48,64,128]{2,1,0:T(8,128)}, u32[]{:S(2)}) copy-start(f32[48,64,128]{2,1,0:T(8,128)} %param.8) | copy-start | bytes 4718596
  203.9 1.1 copy-start.2
  377.0 6.6 %copy-start.3 = (f32[48,64,128]{2,0,1:T(8,128)S(1)}, f32[48,64,128]{2,0,1:T(8,128)}, u32[]{:S(2)}) copy-start(f32[48,64,128]{2,0,1:T(8,128)} %copy-done.2) | copy-start | bytes 4718596
  377.0 6.6 %copy-start.8 = (f32[48,64,128]{2,1,0:T(8,128)S(1)}, f32[48,64,128]{2,1,0:T(8,128)}, u32[]{:S(2)}) copy-start(f32[48,64,128]{2,1,0:T(8,128)} %param.8) | copy-start | bytes 4718596
  388.2 1.1 copy-start
  495.3 58.6 %all-to-all-start.6 = ((bf16[128,2,8192]{2,1,0:T(2,128)(2,1)}), bf16[128,2,8192]{2,1,0:T(2,128)(2,1)}, u32[]{:S(2)}, u32[]{:S(2)}) async-start(bf16[128,2,8192]{2,1,0:T(2,128)(2,1)} %all_to_all.74), calls=%async_computation.6 | async-start | bytes 8388608 | tf_op jit(solution)/shard_map/all_to_all | solution.py:60
  561.2 6.6 %copy-start.1 = (f32[48,64,128]{2,0,1:T(8,128)S(1)}, f32[48,64,128]{2,0,1:T(8,128)}, u32[]{:S(2)}) copy-start(f32[48,64,128]{2,0,1:T(8,128)} %copy-done) | copy-start | bytes 4718596
  561.2 6.6 %copy-start.9 = (f32[48,64,128]{2,1,0:T(8,128)S(1)}, f32[48,64,128]{2,1,0:T(8,128)}, u32[]{:S(2)}) copy-start(f32[48,64,128]{2,1,0:T(8,128)} %param.8) | copy-start | bytes 4718596
where the time goes:
time: 582 us; the launch traced here: 574 us
  blocking collectives  177 us (30%)
  local copies, waits for them, and re-layouts  170 us (29%)
  waiting for transfers between devices  113 us (19%)
  matrix products  78.4 us (13%)
  starting transfers between devices  33.3 us (6%)
    all_to_all x2, blocking collectives, body(): lax.all_to_all(send_tiles, ('sub', 'ifc'), split_axis=0, concat_axis=0, t...  118 us
    all_to_all x2, waiting for transfers between devices, body(): lax.all_to_all(reply, ('sub', 'ifc'), split_axis=0, concat_axis=0, tiled=...  105 us
    all_to_all x9, local copies, waits for them, and re-layouts, body(): lax.all_to_all(reply, ('sub', 'ifc'), split_axis=0, concat_axis=0, tiled=...  64.1 us
    all_to_all x1, blocking collectives, body(): lax.all_to_all(reply, ('sub', 'ifc'), split_axis=0, concat_axis=0, tiled=...  58.8 us
    all_to_all x6, local copies, waits for them, and re-layouts, body(): lax.all_to_all(send_tiles, ('sub', 'ifc'), split_axis=0, concat_axis=0, t...  44.4 us
    dot_general x3, matrix products, body(): jnp.einsum('sij,sjr->sir', schur, gathered, preferred_element_type=jnp.fl...  33.9 us
    unnamed x25, local copies, waits for them, and re-layouts  30.7 us
    gather x1, local copies, waits for them, and re-layouts, body(): jnp.diagonal(schur, axis1=1, axis2=2).astype(jnp.float32)  18.2 us
  transfers between devices with their start and end apart: 4, of which 3 were waited for; matrix products, arithmetic and copies ran while one was open for 12% of the time, Pallas kernels for 0%

commit v1 on v0

v1 whole, which is shorter than its diff:
```python
import functools

import jax
import jax.numpy as jnp
from jax import lax
from jax.experimental import pallas as pl
from jax.experimental.pallas import tpu as pltpu
from jax.sharding import PartitionSpec as P

ITERS = 3
OMEGA = 0.7
MESH = pl.DeviceIdType.MESH
NP = 4
LANES = 128
CAPS = (11, 16)


def kernel(
    cap, tab, s_hbm, lam0, rhs, stiff_t, slot_tile,
    lam, sens,
    s_buf, z, ybf, w, st, run, psum, packed, rc, r1, r2, drow, dsend, drecv, dpart, drc, dx, dfull,
    *rest,
):
    pool, arecv, rrecv = rest[0:NP], rest[NP : 2 * NP], rest[2 * NP : 3 * NP]
    (sem_s, sem_l, g1s, g1r, g2s, g2r, gcs, gcr, as_, ar, bs, br, rcs, rcr, r1s, r1r, r2s, r2r, ds, dr) = rest[3 * NP :]
    nsub, order, _ = s_buf.shape
    nif, tile, width = lam.shape
    rp = tile // NP
    slots = 16 * cap
    half = nif // 2
    line = 4 * nif
    a, b = lax.axis_index("sub"), lax.axis_index("ifc")
    x, y, zz, c = a // 4, a % 4, b // 2, b % 2
    xp, xm, x2 = (x + 1) % 4, (x + 3) % 4, (x + 2) % 4
    j_me = y * 4 + zz
    to_p, to_m, to_2 = (xp * 4 + y, b), (xm * 4 + y, b), (x2 * 4 + y, b)
    to_c = (a, zz * 2 + 1 - c)
    o_t1, o_t2, o_t3 = 0, slots, slots + 96
    o_ord, o_last = 2 * slots + 96, 3 * slots + 96

    def plane(i):
        py, pz = (y + i // 4) % 4, (zz + i % 4) % 4
        return py * 4 + pz, (x * 4 + py, pz * 2 + c)

    def remote(src, dst, ssem, rsem, dev):
        return pltpu.make_async_remote_copy(
            src_ref=src, dst_ref=dst, send_sem=ssem, recv_sem=rsem, device_id=dev, device_id_type=MESH
        )

    def wait_on(ref, sem):
        pltpu.make_async_copy(ref, ref, sem).wait()

    load_s = pltpu.make_async_copy(s_hbm, s_buf, sem_s)
    load_s.start()

    barrier = pltpu.get_barrier_semaphore()
    for dev in (to_p, to_m, to_2, to_c):
        pl.semaphore_signal(barrier, inc=1, device_id=dev, device_id_type=MESH)

    @pl.loop(1, 16)
    def _(i):
        pl.semaphore_signal(barrier, inc=1, device_id=plane(i)[1], device_id_type=MESH)

    @pl.loop(0, nif)
    def _(l):
        lam[l] = lam0[l].astype(jnp.float32)

    pl.semaphore_wait(barrier, 19)

    def at(core, xx, lo=0, n=nif):
        return pl.ds((core * 4 + xx) * nif + lo, n)

    def g0(p):
        rows = slice(p * rp, (p + 1) * rp)
        base = (c * 4 + x) * nif

        @pl.loop(0, nif // 8)
        def _(l):
            pool[p][pl.ds(base + l * 8, 8)] = lam[pl.ds(l * 8, 8), rows].astype(jnp.bfloat16)

        own = pool[p].at[at(c, x)]
        remote(own, own, g1s.at[p, 0], g1r.at[p, 0], to_p).start()
        remote(own, own, g1s.at[p, 1], g1r.at[p, 1], to_m).start()

    def g1(p):
        wait_on(pool[p].at[at(c, xm)], g1r.at[p, 0])
        one = pool[p].at[at(c, xm, 0, half)]
        remote(one, one, g2s.at[p, 0], g2r.at[p, 0], to_p).start()
        wait_on(pool[p].at[at(c, xp)], g1r.at[p, 1])
        two = pool[p].at[at(c, xp, half, half)]
        remote(two, two, g2s.at[p, 1], g2r.at[p, 1], to_m).start()

    def g2(p):
        wait_on(pool[p].at[at(c, x2, 0, half)], g2r.at[p, 0])
        wait_on(pool[p].at[at(c, x2, half, half)], g2r.at[p, 1])
        mine = pool[p].at[pl.ds(c * line, line)]
        remote(mine, mine, gcs.at[p], gcr.at[p], to_c).start()

    def g3(p):
        wait_on(pool[p].at[pl.ds((1 - c) * line, line)], gcr.at[p])

        @pl.loop(0, 16)
        def _(j):
            for k in range(cap):
                q = j * cap + k
                packed[p, q] = pool[p][tab[o_t1 + q]]

        @pl.loop(1, 16)
        def _(i):
            j, dev = plane(i)
            remote(
                packed.at[p, pl.ds(j * cap, cap)], arecv[p].at[pl.ds(j_me * cap, cap)], as_.at[p], ar.at[p], dev
            ).start()

        own = pl.ds(j_me * cap, cap)
        copy = pltpu.make_async_copy(packed.at[p, own], arecv[p].at[own], sem_l)
        copy.start()
        copy.wait()

    def a1(p):
        wait_on(arecv[p].at[pl.ds(0, 15 * cap)], ar.at[p])

        @pl.loop(0, 96 // 8)
        def _(i):
            for u in range(8):
                t = i * 8 + u
                z[t, p * rp : (p + 1) * rp] = arecv[p][tab[o_t2 + t]]

    def multiply(last):
        zz_ = z.reshape(nsub, order, width)
        yy_ = ybf.reshape(nsub, order, width)
        chunk = 256

        @pl.loop(0, nsub)
        def _(s):
            def part(m, acc):
                rows = pl.ds(m * chunk, chunk)
                out = jnp.dot(s_buf[s, rows, :], zz_[s], preferred_element_type=jnp.float32)
                yy_[s, rows, :] = out.astype(jnp.bfloat16)
                prod = out * zz_[s, rows, :].astype(jnp.float32)
                return acc + jnp.sum(prod.reshape(chunk // 8, 8, width), axis=0)

            acc = lax.fori_loop(0, order // chunk, part, jnp.zeros((8, width), jnp.float32))

            @pl.when(last)
            def _():
                sens[s] = -jnp.sum(acc, axis=0, keepdims=True) / order

    def r0(p):
        wait_on(pool[p].at[at(c, x)], g1s.at[p, 0])
        wait_on(pool[p].at[at(c, x)], g1s.at[p, 1])
        wait_on(pool[p].at[at(c, xm, 0, half)], g2s.at[p, 0])
        wait_on(pool[p].at[at(c, xp, half, half)], g2s.at[p, 1])
        wait_on(pool[p].at[pl.ds(c * line, line)], gcs.at[p])
        wait_on(packed.at[p, pl.ds(0, 15 * cap)], as_.at[p])

        @pl.loop(0, 16)
        def _(j):
            for k in range(cap):
                q = j * cap + k
                packed[p, q] = ybf[tab[o_t3 + q], p * rp : (p + 1) * rp]

        @pl.loop(1, 16)
        def _(i):
            j, dev = plane(i)
            remote(
                packed.at[p, pl.ds(j * cap, cap)], rrecv[p].at[pl.ds(j_me * cap, cap)], bs.at[p], br.at[p], dev
            ).start()

        own = pl.ds(j_me * cap, cap)
        copy = pltpu.make_async_copy(packed.at[p, own], rrecv[p].at[own], sem_l)
        copy.start()
        copy.wait()

    def ra(p):
        wait_on(rrecv[p].at[pl.ds(0, 15 * cap)], br.at[p])
        wait_on(packed.at[p, pl.ds(0, 15 * cap)], bs.at[p])

        def add(q8, acc):
            for u in range(8):
                q = q8 * 8 + u
                code = tab[o_ord + q]
                got = rrecv[p][code // 2].astype(jnp.float32)
                acc = jnp.where(code % 2 == 1, 0.0, acc) + got
                run[q] = acc
            return acc

        lax.fori_loop(0, slots // 8, add, jnp.zeros((rp, width), jnp.float32))

        @pl.loop(0, 2 * line // 8)
        def _(t8):
            for u in range(8):
                t = t8 * 8 + u
                pos = tab[o_last + t]
                total = run[jnp.maximum(pos, 0)]
                psum[p, t] = jnp.where(pos >= 0, total, 0.0).astype(jnp.bfloat16)

        remote(psum.at[p, pl.ds((1 - c) * line, line)], rc.at[p], rcs.at[p], rcr.at[p], to_c).start()

    def add_to(p, start, other, n):
        @pl.loop(0, n // 8)
        def _(i):
            here = pl.ds(start + i * 8, 8)
            total = psum[p, here].astype(jnp.float32) + other[pl.ds(i * 8, 8)].astype(jnp.float32)
            psum[p, here] = total.astype(jnp.bfloat16)

    def rb(p):
        wait_on(rc.at[p], rcr.at[p])
        add_to(p, c * line, rc.at[p], line)
        remote(psum.at[p, at(c, x2, 0, half)], r1.at[p, 0], r1s.at[p, 0], r1r.at[p, 0], to_p).start()
        remote(psum.at[p, at(c, x2, half, half)], r1.at[p, 1], r1s.at[p, 1], r1r.at[p, 1], to_m).start()

    def rcc(p):
        wait_on(r1.at[p, 0], r1r.at[p, 0])
        add_to(p, (c * 4 + xp) * nif, r1.at[p, 0], half)
        remote(psum.at[p, at(c, xp)], r2.at[p, 0], r2s.at[p, 0], r2r.at[p, 0], to_p).start()
        wait_on(r1.at[p, 1], r1r.at[p, 1])
        add_to(p, (c * 4 + xm) * nif + half, r1.at[p, 1], half)
        remote(psum.at[p, at(c, xm)], r2.at[p, 1], r2s.at[p, 1], r2r.at[p, 1], to_m).start()

    def rd(p):
        rows = slice(p * rp, (p + 1) * rp)
        wait_on(r2.at[p, 0], r2r.at[p, 0])
        wait_on(r2.at[p, 1], r2r.at[p, 1])
        base = (c * 4 + x) * nif

        @pl.loop(0, nif // 4)
        def _(l4):
            ls = pl.ds(l4 * 4, 4)
            asm = (
                psum[p, pl.ds(base + l4 * 4, 4)].astype(jnp.float32)
                + r2[p, 0, ls].astype(jnp.float32)
                + r2[p, 1, ls].astype(jnp.float32)
            )
            old = lam[ls, rows]
            lam[ls, rows] = old + (rhs[ls, rows] - st[ls, rows] * old - asm) * w[ls, rows]

        wait_on(psum.at[p, pl.ds((1 - c) * line, line)], rcs.at[p])
        wait_on(r1.at[p, 0], r1s.at[p, 0])
        wait_on(r1.at[p, 1], r1s.at[p, 1])
        wait_on(r2.at[p, 0], r2s.at[p, 0])
        wait_on(r2.at[p, 1], r2s.at[p, 1])

    def diag():
        load_s.wait()
        lane = lax.broadcasted_iota(jnp.int32, (tile, LANES), 1)
        row = lax.broadcasted_iota(jnp.int32, (tile, LANES), 0)
        for k in range(order // tile):
            lo = k // 2 * LANES
            keep = lane == row + (k % 2) * tile

            @pl.loop(0, nsub)
            def _(s):
                blk = s_buf[s, k * tile : (k + 1) * tile, lo : lo + LANES].astype(jnp.float32)
                picked = jnp.sum(jnp.where(keep, blk, 0.0), axis=0, keepdims=True)
                if k % 2:
                    picked = pltpu.roll(picked, tile, 1)
                drow[s * (order // tile) + k] = picked

        @pl.loop(0, 16)
        def _(j):
            for k in range(cap):
                dsend[pl.ds(j * 16 + k, 1), :] = drow[tab[o_t3 + j * cap + k]]
            for k in range(cap, 16):
                dsend[pl.ds(j * 16 + k, 1), :] = jnp.zeros((1, LANES), jnp.float32)

        @pl.loop(1, 16)
        def _(i):
            j, dev = plane(i)
            remote(dsend.at[pl.ds(j * 16, 16)], drecv.at[pl.ds(j_me * 16, 16)], ds.at[0], dr.at[0], dev).start()

        own = pl.ds(j_me * 16, 16)
        copy = pltpu.make_async_copy(dsend.at[own], drecv.at[own], sem_l)
        copy.start()
        copy.wait()

    def diag2():
        wait_on(drecv.at[pl.ds(0, 240)], dr.at[0])
        wait_on(dsend.at[pl.ds(0, 240)], ds.at[0])
        came = drecv[...].astype(jnp.bfloat16)
        for h in range(2 * line // LANES):
            want = lax.broadcasted_iota(jnp.int32, (LANES, 256), 0) + h * LANES
            hot = jnp.where(want == slot_tile[...], 1.0, 0.0).astype(jnp.bfloat16)
            dpart[h * LANES : (h + 1) * LANES] = jnp.dot(hot, came, preferred_element_type=jnp.float32)
        remote(dpart.at[pl.ds((1 - c) * line, line)], drc, ds.at[1], dr.at[1], to_c).start()

    def diag3():
        wait_on(drc, dr.at[1])
        mine = pl.ds(c * line, line)
        dpart[mine] += drc[...]
        wait_on(drc, ds.at[1])
        for i, (xt, dev) in enumerate(((xp, to_p), (xm, to_m), (x2, to_2))):
            remote(dpart.at[at(c, xt)], dx.at[i], ds.at[2 + i], dr.at[2 + i], dev).start()

    def diag4():
        for i in range(3):
            wait_on(dx.at[i], dr.at[2 + i])
        dfull[...] = jnp.zeros_like(dfull)
        dfull[0:nif] = dpart[at(c, x)] + dx[0] + dx[1] + dx[2]
        for i in range(3):
            wait_on(dx.at[i], ds.at[2 + i])
        stt = stiff_t[...]
        inv = OMEGA / (stt + dfull[...].T[0:tile])
        for g in range(nif):
            w[g] = jnp.broadcast_to(inv[:, g : g + 1], (tile, width))
            st[g] = jnp.broadcast_to(stt[:, g : g + 1], (tile, width))

    for p in range(NP):
        g0(p)
    diag()
    diag2()
    diag3()
    diag4()

    @pl.loop(0, ITERS)
    def _(sweep):
        for t in range(NP + 3):
            for j, stage in reversed(list(enumerate((g1, g2, g3, a1)))):
                if 0 <= t - j < NP:
                    stage(t - j)
        multiply(sweep == ITERS - 1)
        for p in range(NP):
            r0(p)

        def rd_g0(p):
            rd(p)

            @pl.when(sweep < ITERS - 1)
            def _():
                g0(p)

        for t in range(NP + 3):
            for j, stage in reversed(list(enumerate((ra, rb, rcc, rd_g0)))):
                if 0 <= t - j < NP:
                    stage(t - j)


def sweeps(cap, cid, schur, lam_start, rhs, stiff, all_owner, all_local):
    nsub, order, _ = schur.shape
    nif, tile, width = lam_start.shape
    i32 = jnp.int32
    a, b = lax.axis_index("sub"), lax.axis_index("ifc")
    x, y, zz, c = a // 4, a % 4, b // 2, b % 2
    j_me = y * 4 + zz
    me = a * 8 + b
    slots = 16 * cap

    grid = (4, 4, 4, 2, 96)
    own5 = lax.dynamic_slice(all_owner.reshape(grid), (x, 0, 0, c, 0), (1, 4, 4, 1, 96)).reshape(16, 96)
    loc5 = lax.dynamic_slice(all_local.reshape(grid), (x, 0, 0, c, 0), (1, 4, 4, 1, 96)).reshape(16, 96)
    here = (own5 // 2) % 16 == j_me
    before = jnp.arange(96)[:, None] < jnp.arange(96)[None, :]
    rank = jnp.sum((here[:, :, None] & before[None]).astype(i32), axis=1)
    tid = ((own5 % 2) * 4 + own5 // 32) * nif + loc5
    match = here[:, :, None] & (rank[:, :, None] == jnp.arange(cap)[None, None, :])
    slot_tile = jnp.sum(jnp.where(match, tid[:, :, None] + 1, 0), axis=1) - 1
    flat = slot_tile.reshape(slots)
    t1 = jnp.maximum(flat, 0)
    seat = jnp.arange(slots)
    val = jnp.where(flat < 0, 8 * nif, flat)
    key = val * 256 + seat
    pos = jnp.sum((key[None, :] < key[:, None]).astype(i32), axis=1)
    first = ~jnp.any((val[None, :] == val[:, None]) & (seat[None, :] < seat[:, None]), axis=1)
    code = seat * 2 + first.astype(i32)
    order_tab = jnp.sum(jnp.where(pos[:, None] == seat[None, :], code[:, None], 0), axis=0)
    tiles = jnp.arange(8 * nif)
    upto = jnp.sum((val[None, :] <= tiles[:, None]).astype(i32), axis=1)
    has = jnp.any(val[None, :] == tiles[:, None], axis=1)
    last = jnp.where(has, upto - 1, -1)

    mine = lax.dynamic_slice_in_dim(all_owner, me, 1, 0)[0]
    group = (mine // 2) % 16
    same = (group[None, :] == group[:, None]) & (jnp.arange(96)[None, :] < jnp.arange(96)[:, None])
    t2 = group * cap + jnp.sum(same.astype(i32), axis=1)
    t3 = jnp.sum(jnp.where(t2[:, None] == seat[None, :], jnp.arange(96)[:, None], 0), axis=0)
    tab = jnp.concatenate([t1, t2, t3, order_tab, last]).astype(i32)
    wide = jnp.pad(slot_tile, ((0, 0), (0, 16 - cap)), constant_values=-1).reshape(1, 256)
    stiff_t = jnp.pad(stiff, ((0, LANES - nif), (0, 0)), constant_values=1.0).T

    rp = tile // NP
    bf, f32 = jnp.bfloat16, jnp.float32
    vm = pltpu.VMEM
    dma = pltpu.SemaphoreType.DMA
    line = 4 * nif
    scratch = [
        vm((nsub, order, order), bf),
        vm((96, tile, width), bf),
        vm((96, tile, width), bf),
        vm((nif, tile, width), f32),
        vm((nif, tile, width), f32),
        vm((slots, rp, width), f32),
        vm((NP, 2 * line, rp, width), bf),
        vm((NP, slots, rp, width), bf),
        vm((NP, line, rp, width), bf),
        vm((NP, 2, nif // 2, rp, width), bf),
        vm((NP, 2, nif, rp, width), bf),
        vm((96, 1, LANES), f32),
        vm((256, LANES), f32),
        vm((256, LANES), f32),
        vm((2 * line, LANES), f32),
        vm((line, LANES), f32),
        vm((3, nif, LANES), f32),
        vm((LANES, LANES), f32),
    ]
    scratch += [vm((2 * line, rp, width), bf)] * NP
    scratch += [vm((slots, rp, width), bf)] * (2 * NP)
    scratch += [dma, dma]
    scratch += [dma((NP, 2))] * 4 + [dma((NP,))] * 8 + [dma((NP, 2))] * 4 + [dma((5,))] * 2
    in_vm = pl.BlockSpec(memory_space=vm)
    lam, sens = pl.pallas_call(
        functools.partial(kernel, cap),
        out_shape=(
            jax.ShapeDtypeStruct((nif, tile, width), f32),
            jax.ShapeDtypeStruct((nsub, 1, width), f32),
        ),
        in_specs=[pl.BlockSpec(memory_space=pltpu.SMEM), pl.BlockSpec(memory_space=pl.ANY), in_vm, in_vm, in_vm, in_vm],
        out_specs=(in_vm, in_vm),
        scratch_shapes=scratch,
        compiler_params=pltpu.CompilerParams(
            collective_id=cid, has_side_effects=True, vmem_limit_bytes=63 * 2**20
        ),
        name=f"sweeps_{cap}",
    )(tab, schur, lam_start, rhs, stiff_t, wide)
    return lam, sens.reshape(nsub, width)


def body(schur, lam_start, rhs, stiff, owner, local):
    all_owner = owner.reshape(128, 96)
    all_local = local.reshape(128, 96)
    group = (all_owner // 2) % 16
    most = jnp.max(jnp.sum((group[:, :, None] == jnp.arange(16)).astype(jnp.int32), axis=1))
    args = (schur, lam_start, rhs, stiff, all_owner, all_local)
    return lax.cond(
        most <= CAPS[0],
        functools.partial(sweeps, CAPS[0], 0),
        functools.partial(sweeps, CAPS[1], 1),
        *args,
    )


def solution(mesh):
    spec = P(("sub", "ifc"), None, None)
    return jax.shard_map(
        body,
        mesh=mesh,
        in_specs=(spec, spec, spec, P(("sub", "ifc"), None), P(), P()),
        out_specs=(spec, P(("sub", "ifc"), None)),
        check_vma=False,
    )
```

time: 582 us -> 411 us (0.71); the launches traced: 574 us -> 410 us
  Pallas kernels: 0 us -> 397 us
  blocking collectives: 177 us -> 0 us
  local copies, waits for them, and re-layouts: 170 us -> 9.51 us
  waiting for transfers between devices: 113 us -> 0 us
  matrix products: 78.4 us -> 0 us
  starting transfers between devices: 33.3 us -> 0 us
    pallas_call x0 -> x1, Pallas kernels: none -> 397 us  [sweeps(): pl.pallas_call(functools.partial(kernel, cap), out_shape=(jax.ShapeDtypeS...]
    all_to_all x3 -> x0, blocking collectives: 177 us -> none  [the longest x2 118 us: body(): lax.all_to_all(send_tiles, ('sub', 'ifc'), split_axis=0, concat_axis=0, t...]
    all_to_all x4 -> x0, waiting for transfers between devices: 113 us -> none  [the longest x2 105 us: body(): lax.all_to_all(reply, ('sub', 'ifc'), split_axis=0, concat_axis=0, tiled=...]
    all_to_all x15 -> x0, local copies, waits for them, and re-layouts: 108 us -> none  [the longest x9 64.1 us: body(): lax.all_to_all(reply, ('sub', 'ifc'), split_axis=0, concat_axis=0, tiled=...]
    dot_general x17 -> x0, matrix products: 78.4 us -> none  [the longest x3 33.9 us: body(): jnp.einsum('sij,sjr->sir', schur, gathered, preferred_element_type=jnp.fl...]
    all_to_all x4 -> x0, starting transfers between devices: 33.3 us -> none  [the longest x2 16 us: body(): lax.all_to_all(reply, ('sub', 'ifc'), split_axis=0, concat_axis=0, tiled=...]
    unnamed x25 -> x3, local copies, waits for them, and re-layouts: 30.7 us -> 4.23 us
    gather x1 -> x0, local copies, waits for them, and re-layouts: 18.2 us -> none  [body(): jnp.diagonal(schur, axis1=1, axis2=2).astype(jnp.float32)]
  transfers between devices with their start and end apart: 4 -> 0, of which waited for: 3 -> 0; matrix products, arithmetic and copies ran while one was open for 12% -> 0% of each run, Pallas kernels for 0% -> 0%
where the time goes in v1:
time: 411 us; the launch traced here: 410 us
  Pallas kernels  397 us (97%)
  local copies, waits for them, and re-layouts  9.51 us (2%)
    pallas_call x1, Pallas kernels, sweeps(): pl.pallas_call(functools.partial(kernel, cap), out_shape=(jax.ShapeDtypeS...  397 us

profile of v1, /device:TPU:1, one launch (start us, length us, event | category | flops | bytes accessed | tf_op | source)
XLA Modules:
  0.0 410.2 jit_solution(1096146474977265362)
XLA Ops:
  0.6 0.9 copy.31
  1.6 0.1 reshape.474
  1.7 0.1 add_select_fusion.10
  1.8 0.1 copy.32
  1.8 0.1 convert_reduce_fusion.8
  2.0 0.6 reduce_max.9
  3.3 403.6 %conditional.1 = (f32[48,64,128]{2,1,0:T(8,128)}, f32[4,128]{1,0:T(4,128)S(1)}) conditional(s32[]{:T(128)} %convert_element_type.45, (s32[512,24,1]{0,2,1:T(1,128)}, s32[512,24]{0,1:T(8,128)}, s32[128,96]{1,0:T(8,128)S(1)}, f32[48,64]{1,0:T(8,128)}, bf16[4,1536,1536]{2,1,0:T(8,128)(2,1)}, /*index=5*/bf16[48,64,128]{2,1,0:T(8,128)(2,1)}, ...), branch_computations={%region_2.12_spmd, %region_12.22_spmd} | conditional | flops 1908440 | bytes 3741444 | solution.py:433
  3.3 0.0 copy-start.1
  3.4 0.2 convert_reduce_fusion.7
  3.6 0.1 select_reduce_fusion.4
  3.8 0.8 copy.38
  4.6 0.6 pad_bitcast_fusion.1.stiff_t
  5.2 0.9 copy.37
  6.1 0.1 reshape_reshape.11
  6.3 0.9 copy.36
  7.2 0.1 reshape_reshape.10
  7.4 0.3 convert_reduce_fusion.4
  7.7 0.3 select_reduce_fusion.5
  8.0 0.1 copy.29
  8.1 0.1 sub.64
  8.2 0.6 reshape.471.slot_tile
  8.9 0.2 convert_reduce_fusion.6
  9.0 0.2 fusion.23
  9.2 0.1 select_reduce_fusion.3
  9.4 0.1 fusion.21
  9.5 0.1 convert_reduce_fusion.5
  9.6 0.7 concatenate.5.tab
  10.3 0.0 copy-done.1
  10.3 396.6 %sweeps_11.1 = (f32[48,64,128]{2,1,0:T(8,128)}, f32[4,1,128]{2,1,0:T(1,128)S(1)}) custom-call(s32[1008]{0:T(1024)} %concatenate.5.tab, bf16[4,1536,1536]{2,1,0:T(8,128)(2,1)} %get-tuple-element.40.s_hbm, bf16[48,64,128]{2,1,0:T(8,128)(2,1)S(1)} %copy-done.1, f32[48,64,128]{2,1,0:T(8,128)} %get-tuple-element.42.rhs, f32[64,128]{1,0:T(8,128)} %pad_bitcast_fusion.1.stiff_t, ...), custom_call_target="tpu_custom_call" | custom-call | tf_op jit(solution)/shard_map/cond/branch_1_fun/sweeps_11/pallas_call | solution.py:410
  406.9 2.7 copy.46
  409.6 0.6 copy.47
  (12 shorter events, 0.2 us)
Async XLA Ops:
  3.3 7.0 %copy-start.1 = (bf16[48,64,128]{2,1,0:T(8,128)(2,1)S(1)}, bf16[48,64,128]{2,1,0:T(8,128)(2,1)}, u32[]{:S(2)}) copy-start(bf16[48,64,128]{2,1,0:T(8,128)(2,1)} %get-tuple-element.41.lam0) | copy-start | bytes 2359300 | tf_op jit(solution)/shard_map/cond
